TPU v7x, 32 devices: a whole 2x2x4 slice. The times are simulated.
32 devices in a mesh: dom: 8 (over z, y), serve: 4 (over x, core).
Axes of the slice: x: 2, y: 2, z: 4, core: 2. Of those that a mesh axis runs over, the one named last changes fastest.
Arguments:
- source_rows: float32 [8, 4, 256, 400], P('dom', 'serve'), may hold values from -1.5 to 1.5
- source_state: float32 [8, 4, 256], P('dom', 'serve'), may hold values from 0.01 to 1
- target_rows: float32 [8, 4, 256, 400], P('dom', 'serve'), may hold values from -1.5 to 1.5
- target_state: float32 [8, 4, 256], P('dom', 'serve'), may hold values from 0.01 to 1
- relation_table: float32 [16, 400], replicated, may hold values from -4 to 4
- source_ids: int32 [8, 4, 2, 8, 128], P('dom', 'serve'), may hold values from 0 to 255
- target_ids: int32 [8, 4, 2, 8, 128], P('dom', 'serve'), may hold values from 0 to 255
- relation_ids: int32 [8, 4, 2, 8, 128], P('dom', 'serve'), may hold values from 0 to 15
- negative_block: int32 [8, 4, 2, 8], P('dom', 'serve'), may hold values from 0 to 1
- edge_counts: int32 [8, 4, 2, 8], P('dom', 'serve'), may hold values from 1 to 128, 768 in all within a row
- serving_shard: int32 [8, 4, 256], P('dom', 'serve'), may hold values from 0 to 3
- changed_rows: int32 [8, 4, 256], P('dom', 'serve'), may hold values from 0 to 1, as said below
Outputs:
- new_source: float32 [8, 4, 256, 400], P('dom', 'serve')
- new_source_state: float32 [8, 4, 256], P('dom', 'serve')
- new_target: float32 [8, 4, 256, 400], P('dom', 'serve')
- new_target_state: float32 [8, 4, 256], P('dom', 'serve')
- served: bfloat16 [8, 4, 4, 256, 400], P('dom', 'serve')
Inputs may be any that keep to these rules, and one draw needn't show every extreme that they name: `edge_counts`: for one device and step, the 8 counts sum to 768 and the largest is exactly 128. `changed_rows`: on every device at most 64 changed rows have one serving shard, and exactly 64 have some shard, the same shard for all devices of one index of dom.
All inputs are finite; a program needn't handle non-finite values.
Results may differ from a plain program's by a relative error of at most 0.001.
Values may be sent and summed in bfloat16 or wider, within the bound.
A program may use at most 64 MiB of HBM per device.

v0:
```python
import functools
import jax
import jax.numpy as jnp
from jax import lax
from jax.experimental import pallas as pl
from jax.experimental.pallas import tpu as pltpu
from jax.sharding import PartitionSpec as P

LEARN_RATE = 0.1
EPSILON = 1e-08
BLOCK = 128
CHUNK = 256
MESH = pl.DeviceIdType.MESH
F32 = jnp.float32
BF16 = jnp.bfloat16


def dot(a, b, contract=((1,), (0,))):
    return lax.dot_general(a, b, (contract, ((), ())), preferred_element_type=F32)


def split(x):
    high = x.astype(BF16)
    return high, (x - high.astype(F32)).astype(BF16)


def down(row):
    return jnp.broadcast_to(row, (BLOCK, BLOCK)).T


def column(row):
    return jnp.broadcast_to(row, (8, row.shape[1])).T[:, :1]


def as_row(col):
    return jnp.broadcast_to(col, (col.shape[0], BLOCK)).T[:1, :]


def adagrad(weights, state_col, grad):
    state_col = state_col + jnp.mean(grad * grad, axis=-1, keepdims=True)
    rate = LEARN_RATE / (jnp.sqrt(state_col) + EPSILON)
    return weights - rate * grad, state_col


def kernel(
    dom, serve, steps, blocks,
    src, sst, tgt, tst, rel, sid, tid, rid, nb, cnt, shard, changed,
    o_src, o_sst, o_tgt, o_tst, o_served,
    ubuf, unew, mbuf, msend, code, code_in, pay, pay_in, expand,
    rstack, relg, qhi, qlo, whi, wlo,
    u_send, u_recv, m_send, m_recv, c_send, c_recv, p_send, p_recv,
):
    rows, width = src.shape
    nrel = rel.shape[0]
    chunks = blocks * BLOCK // CHUNK
    per = CHUNK // BLOCK
    slots = pay.shape[1]
    d = lax.axis_index("dom")
    s = lax.axis_index("serve")
    right, left = lax.rem(d + 1, dom), lax.rem(d + dom - 1, dom)
    peers = [lax.rem(s + j, serve) for j in range(1, serve)]

    barrier = pltpu.get_barrier_semaphore()
    for neighbour in (left, right):
        pl.semaphore_signal(barrier, inc=1, device_id=(neighbour, s), device_id_type=MESH)
    for peer in peers:
        pl.semaphore_signal(barrier, inc=1, device_id=(d, peer), device_id_type=MESH)
    msend[0] = jnp.broadcast_to(tst[...], (8, rows))
    code[...] = jnp.broadcast_to(
        jnp.where(changed[...] == 1, shard[...], -1).astype(F32), (8, rows)
    )
    pl.semaphore_wait(barrier, 2 + serve - 1)

    def ring(step, rows_ref):
        u = pltpu.make_async_remote_copy(
            src_ref=rows_ref, dst_ref=ubuf.at[step], send_sem=u_send.at[step],
            recv_sem=u_recv.at[step], device_id=(right, s), device_id_type=MESH)
        m = pltpu.make_async_remote_copy(
            src_ref=msend.at[step], dst_ref=mbuf.at[step], send_sem=m_send.at[step],
            recv_sem=m_recv.at[step], device_id=(right, s), device_id_type=MESH)
        u.start()
        m.start()
        return u, m

    moving = ring(0, tgt)
    code_copies = []
    for j, peer in enumerate(peers):
        c = pltpu.make_async_remote_copy(
            src_ref=code, dst_ref=code_in.at[j], send_sem=c_send.at[j],
            recv_sem=c_recv.at[j], device_id=(d, peer), device_id_type=MESH)
        c.start()
        code_copies.append(c)

    lane = lax.broadcasted_iota(jnp.int32, (CHUNK, BLOCK), 1).astype(F32)
    lane_rows = lax.broadcasted_iota(jnp.int32, (CHUNK, rows), 1)
    lane_rows_f = lane_rows.astype(F32)
    edge = lax.broadcasted_iota(jnp.int32, (CHUNK, 1), 0)
    sub_rows = lax.broadcasted_iota(jnp.int32, (rows, BLOCK), 0).astype(F32)

    def ids_down(ref, step, c):
        parts = [
            down(ref[step, c * per + i : c * per + i + 1, :].astype(F32)) for i in range(per)
        ]
        return jnp.concatenate(parts, axis=0)

    def one_hot(ids):
        wide = jnp.concatenate([ids] * (rows // BLOCK), axis=1)
        return wide == lane_rows_f

    def one_hot_t(ref, step, c):
        parts = [
            jnp.where(
                sub_rows == ref[step, c * per + i : c * per + i + 1, :].astype(F32), 1.0, 0.0
            ).astype(BF16)
            for i in range(per)
        ]
        return jnp.concatenate(parts, axis=1)

    rstack[...] = jnp.zeros_like(rstack)
    first, rest = rel[...], rel[...]
    for i in range(3):
        part = first.astype(BF16)
        rstack[i * nrel : (i + 1) * nrel, :] = part
        first = first - part.astype(F32)
    lane_i = lax.broadcasted_iota(jnp.int32, (CHUNK, BLOCK), 1)
    lane_rel = jnp.where(lane_i < 3 * nrel, lax.rem(lane_i, nrel), -1).astype(F32)

    def relations(step):
        for c in range(chunks):
            hot = jnp.where(ids_down(rid, step, c) == lane_rel, 1.0, 0.0).astype(BF16)
            at = (step * chunks + c) * CHUNK
            relg[at : at + CHUNK, :] = dot(hot, rstack[...])

    def queries(step, source):
        high, low = split(source)
        for c in range(chunks):
            hot = jnp.where(one_hot(ids_down(sid, step, c)), 1.0, 0.0).astype(BF16)
            rows_of = dot(hot, high) + dot(hot, low)
            at = (step * chunks + c) * CHUNK
            q_high, q_low = split(rows_of * relg[at : at + CHUNK, :])
            qhi[c * CHUNK : (c + 1) * CHUNK, :] = q_high
            qlo[c * CHUNK : (c + 1) * CHUNK, :] = q_low

    def weights(step, u_high, u_low):
        for c in range(chunks):
            at = slice(c * CHUNK, (c + 1) * CHUNK)
            a, b = qhi[at, :], qlo[at, :]
            nt = ((1,), (1,))
            logits = dot(a, u_high, nt) + dot(a, u_low, nt) + dot(b, u_high, nt)
            hot = one_hot(ids_down(tid, step, c))
            count = cnt[step, c * per]
            block = nb[step, c * per]
            for i in range(1, per):
                count = jnp.where(edge >= i * BLOCK, cnt[step, c * per + i] + i * BLOCK, count)
                block = jnp.where(edge >= i * BLOCK, nb[step, c * per + i], block)
            valid = jnp.where(edge < count, 1.0, 0.0)
            pos = jnp.sum(jnp.where(hot, logits, 0.0), axis=1, keepdims=True)
            dpos = -jax.nn.sigmoid(-pos) * valid
            negative = (lane_rows // BLOCK) == block
            dneg = jnp.where(negative, jax.nn.sigmoid(logits) * (valid / BLOCK), 0.0)
            w_high, w_low = split(jnp.where(hot, dpos, 0.0) + dneg)
            whi[at, :] = w_high
            wlo[at, :] = w_low

    def target_grad():
        total = jnp.zeros((rows, width), F32)
        for c in range(chunks):
            at = slice(c * CHUNK, (c + 1) * CHUNK)
            tn = ((0,), (0,))
            total += dot(whi[at, :], qhi[at, :], tn)
            total += dot(wlo[at, :], qhi[at, :], tn)
            total += dot(whi[at, :], qlo[at, :], tn)
        return total

    def source_grad(step, u_high, u_low):
        total = jnp.zeros((rows, width), F32)
        for c in range(chunks):
            at = slice(c * CHUNK, (c + 1) * CHUNK)
            g = dot(whi[at, :], u_high) + dot(wlo[at, :], u_high) + dot(whi[at, :], u_low)
            r = (step * chunks + c) * CHUNK
            g_high, g_low = split(g * relg[r : r + CHUNK, :])
            hot = one_hot_t(sid, step, c)
            total += dot(hot, g_high) + dot(hot, g_low)
        return total

    def compaction(code_row, which):
        sel = jnp.where(code_row == which.astype(F32), 1.0, 0.0)
        before = lax.broadcasted_iota(jnp.int32, (rows, rows), 0)
        after = lax.broadcasted_iota(jnp.int32, (rows, rows), 1)
        tri = jnp.where(before < after, 1.0, 0.0).astype(BF16)
        rank = dot(jnp.broadcast_to(sel, (16, rows)).astype(BF16), tri)[:1, :]
        slot = lax.broadcasted_iota(jnp.int32, (slots, rows), 0).astype(F32)
        return jnp.where((rank == slot) & (sel > 0.0), 1.0, 0.0)

    for step in range(steps):
        relations(step)
    source, source_state = src[...], column(sst[...])
    queries(0, source)
    for j in range(serve - 1):
        code_copies[j].wait()
        expand[j] = compaction(code_in[j, :1, :], s).T.astype(BF16)

    target = None
    for step in range(steps):
        last = step == steps - 1
        for copy in moving:
            copy.wait()
        target = ubuf[step]
        target_state = column(mbuf[step, :1, :])
        u_high, u_low = split(target)
        weights(step, u_high, u_low)
        if not last:
            target, target_state = adagrad(target, target_state, target_grad())
            unew[step] = target
            msend[step + 1] = jnp.broadcast_to(as_row(target_state), (8, rows))
            moving = ring(step + 1, unew.at[step])
            source, source_state = adagrad(
                source, source_state, source_grad(step, u_high, u_low))
            queries(step + 1, source)
        else:
            source, source_state = adagrad(
                source, source_state, source_grad(step, u_high, u_low))
            published = source.astype(BF16)
            pay_copies = []
            for j, peer in enumerate(peers):
                pick = compaction(code[:1, :], peer).astype(BF16)
                pay[j] = dot(pick, published).astype(BF16)
                p = pltpu.make_async_remote_copy(
                    src_ref=pay.at[j], dst_ref=pay_in.at[j], send_sem=p_send.at[j],
                    recv_sem=p_recv.at[j], device_id=(d, peer), device_id_type=MESH)
                p.start()
                pay_copies.append(p)
            target, target_state = adagrad(target, target_state, target_grad())
            o_tgt[...] = target
            o_tst[...] = as_row(target_state)
            o_src[...] = source
            o_sst[...] = as_row(source_state)
            own = column(code[:1, :]) == s.astype(F32)
            o_served[s] = jnp.where(own, source, 0.0).astype(BF16)
            for j in range(serve - 1):
                pay_copies[j].wait()
                sender = lax.rem(s + serve - 1 - j, serve)
                o_served[sender] = dot(expand[j], pay_in[j]).astype(BF16)


def on_device(
    dom, serve,
    source_rows, source_state, target_rows, target_state, relation_table,
    source_ids, target_ids, relation_ids, negative_block, edge_counts,
    serving_shard, changed_rows,
):
    _, _, rows, width = source_rows.shape
    _, _, steps, blocks, _ = source_ids.shape
    nrel = relation_table.shape[0]
    slots = rows // 4
    edges = blocks * BLOCK
    vmem = pl.BlockSpec(memory_space=pltpu.VMEM)
    smem = pl.BlockSpec(memory_space=pltpu.SMEM)
    dma = pltpu.SemaphoreType.DMA
    outs = pl.pallas_call(
        functools.partial(kernel, dom, serve, steps, blocks),
        out_shape=(
            jax.ShapeDtypeStruct((rows, width), F32),
            jax.ShapeDtypeStruct((1, rows), F32),
            jax.ShapeDtypeStruct((rows, width), F32),
            jax.ShapeDtypeStruct((1, rows), F32),
            jax.ShapeDtypeStruct((serve, rows, width), BF16),
        ),
        in_specs=[vmem] * 8 + [smem] * 2 + [vmem] * 2,
        out_specs=(vmem,) * 5,
        scratch_shapes=[
            pltpu.VMEM((steps, rows, width), F32),
            pltpu.VMEM((steps, rows, width), F32),
            pltpu.VMEM((steps, 8, rows), F32),
            pltpu.VMEM((steps, 8, rows), F32),
            pltpu.VMEM((8, rows), F32),
            pltpu.VMEM((serve - 1, 8, rows), F32),
            pltpu.VMEM((serve - 1, slots, width), BF16),
            pltpu.VMEM((serve - 1, slots, width), BF16),
            pltpu.VMEM((serve - 1, rows, slots), BF16),
            pltpu.VMEM((BLOCK, width), BF16),
            pltpu.VMEM((steps * edges, width), F32),
            pltpu.VMEM((edges, width), BF16),
            pltpu.VMEM((edges, width), BF16),
            pltpu.VMEM((edges, rows), BF16),
            pltpu.VMEM((edges, rows), BF16),
            dma((steps,)), dma((steps,)), dma((steps,)), dma((steps,)),
            dma((serve - 1,)), dma((serve - 1,)), dma((serve - 1,)), dma((serve - 1,)),
        ],
        compiler_params=pltpu.CompilerParams(
            collective_id=0, has_side_effects=True, vmem_limit_bytes=48 * 1024 * 1024
        ),
        name="train_and_publish",
    )(
        source_rows[0, 0], source_state[0], target_rows[0, 0], target_state[0],
        relation_table, source_ids[0, 0], target_ids[0, 0], relation_ids[0, 0],
        negative_block[0, 0], edge_counts[0, 0], serving_shard[0], changed_rows[0],
    )
    source, source_sums, target, target_sums, served = outs
    return (source[None, None], source_sums[None], target[None, None], target_sums[None],
            served[None, None])


def solution(mesh):
    rows4 = P("dom", "serve", None, None)
    rows3 = P("dom", "serve", None)
    ids = P("dom", "serve", None, None, None)
    return jax.shard_map(
        functools.partial(on_device, mesh.shape["dom"], mesh.shape["serve"]),
        mesh=mesh,
        in_specs=(rows4, rows3, rows4, rows3, P(), ids, ids, ids, rows4, rows4, rows3, rows3),
        out_specs=(rows4, rows3, rows4, rows3, ids),
        check_vma=False,
    )
```

profile of v0, /device:TPU:1, one launch (start us, length us, event | category | flops | bytes accessed | tf_op | source)
XLA Modules:
  0.0 48.8 jit_solution(6314422254411977278)
XLA Ops:
  0.6 0.0 copy-start.10
  0.6 1.2 %copy.17 = f32[1,1,256,400]{3,2,1,0:T(8,128)S(1)} copy(f32[1,1,256,400]{2,3,1,0:T(8,128)} %param.12) | data formatting | bytes 819200 | tf_op args[0]
  1.9 0.0 copy-done.10
  1.9 0.0 copy-start
  1.9 0.0 copy-start.1
  1.9 0.0 copy-start.2
  1.9 0.0 copy-start.3
  2.0 0.0 copy-start.5
  2.0 0.0 copy-start.6
  2.0 0.0 copy-start.7
  2.0 0.0 copy-start.8
  2.0 0.0 copy-start.9
  2.0 0.2 copy.18
  2.2 0.0 copy-start.4
  2.2 0.4 copy-done
  2.7 0.0 copy-done.1
  2.7 0.0 copy-done.2
  2.7 0.0 copy-done.3
  2.7 0.0 copy-done.5
  2.7 0.0 copy-done.6
  2.7 0.0 copy-done.7
  2.7 0.0 copy-done.8
  2.7 0.0 copy-done.9
  2.7 0.2 copy-done.4
  2.9 41.7 %train_and_publish.1 = (f32[256,400]{1,0:T(8,128)S(1)}, f32[1,256]{1,0:T(1,128)S(1)}, f32[256,400]{1,0:T(8,128)S(1)}, f32[1,256]{1,0:T(1,128)S(1)}, bf16[4,256,400]{2,1,0:T(8,128)(2,1)S(1)}) custom-call(f32[256,400]{1,0:T(8,128)S(1)} %bitcast.16, f32[1,256]{1,0:T(1,128)S(1)} %bitcast.26, f32[256,400]{1,0:T(8,128)S(1)} %bitcast.17, f32[1,256]{1,0:T(1,128)S(1)} %bitcast.27, ...), custom_call_target="tpu_custom_call" | custom-call | tf_op jit(solution)/shard_map/train_and_publish/pallas_call | solution.py:260
  44.6 0.9 %copy.19 = f32[1,1,256,400]{2,3,1,0:T(8,128)} copy(f32[1,1,256,400]{3,2,1,0:T(8,128)S(1)} %bitcast.20) | data formatting | bytes 819200
  45.5 0.9 %copy.20 = f32[1,1,256,400]{2,3,1,0:T(8,128)} copy(f32[1,1,256,400]{3,2,1,0:T(8,128)S(1)} %bitcast.19) | data formatting | bytes 819200
  46.5 1.3 %copy.21 = bf16[1,1,4,256,400]{3,4,2,1,0:T(8,128)(2,1)} copy(bf16[1,1,4,256,400]{4,3,2,1,0:T(8,128)(2,1)S(1)} %bitcast.18) | data formatting | bytes 1638400
  47.7 0.6 %copy.24 = f32[1,1,256]{2,1,0:T(1,128)} copy(f32[1,1,256]{2,1,0:T(1,128)S(1)} %bitcast.25) | data formatting | bytes 2048
  48.3 0.6 %copy.25 = f32[1,1,256]{2,1,0:T(1,128)} copy(f32[1,1,256]{2,1,0:T(1,128)S(1)} %bitcast.24) | data formatting | bytes 2048
Async XLA Ops:
  0.6 1.3 %copy-start.10 = (f32[1,1,256,400]{2,3,1,0:T(8,128)S(1)}, f32[1,1,256,400]{2,3,1,0:T(8,128)}, u32[]{:S(2)}) copy-start(f32[1,1,256,400]{2,3,1,0:T(8,128)} %param.14) | copy-start | bytes 1228804
  1.9 0.8 %copy-start = (f32[16,400]{1,0:T(8,128)S(1)}, f32[16,400]{1,0:T(8,128)}, u32[]{:S(2)}) copy-start(f32[16,400]{1,0:T(8,128)} %rel.1) | copy-start | bytes 76804
  1.9 0.8 %copy-start.1 = (s32[1,1,2,8,128]{4,3,2,1,0:T(8,128)S(1)}, s32[1,1,2,8,128]{4,3,2,1,0:T(8,128)}, u32[]{:S(2)}) copy-start(s32[1,1,2,8,128]{4,3,2,1,0:T(8,128)} %param.17) | copy-start | bytes 24580
  1.9 0.7 %copy-start.2 = (s32[1,1,2,8,128]{4,3,2,1,0:T(8,128)S(1)}, s32[1,1,2,8,128]{4,3,2,1,0:T(8,128)}, u32[]{:S(2)}) copy-start(s32[1,1,2,8,128]{4,3,2,1,0:T(8,128)} %param.18) | copy-start | bytes 24580
  1.9 0.7 %copy-start.3 = (s32[1,1,2,8,128]{4,3,2,1,0:T(8,128)S(1)}, s32[1,1,2,8,128]{4,3,2,1,0:T(8,128)}, u32[]{:S(2)}) copy-start(s32[1,1,2,8,128]{4,3,2,1,0:T(8,128)} %param.19) | copy-start | bytes 24580
  2.0 0.7 %copy-start.5 = (f32[1,1,256]{2,1,0:T(1,128)S(1)}, f32[1,1,256]{2,1,0:T(1,128)}, u32[]{:S(2)}) copy-start(f32[1,1,256]{2,1,0:T(1,128)} %param.15) | copy-start | bytes 3076
  2.0 0.7 %copy-start.6 = (s32[1,1,2,8]{3,2,1,0:T(2,128)S(1)}, s32[1,1,2,8]{3,2,1,0:T(2,128)}, u32[]{:S(2)}) copy-start(s32[1,1,2,8]{3,2,1,0:T(2,128)} %param.20) | copy-start | bytes 196
  2.0 0.7 %copy-start.7 = (s32[1,1,2,8]{3,2,1,0:T(2,128)S(1)}, s32[1,1,2,8]{3,2,1,0:T(2,128)}, u32[]{:S(2)}) copy-start(s32[1,1,2,8]{3,2,1,0:T(2,128)} %param.21) | copy-start | bytes 196
  2.0 0.7 %copy-start.8 = (s32[1,1,256]{2,1,0:T(1,128)S(1)}, s32[1,1,256]{2,1,0:T(1,128)}, u32[]{:S(2)}) copy-start(s32[1,1,256]{2,1,0:T(1,128)} %param.22) | copy-start | bytes 3076
  2.0 0.7 %copy-start.9 = (s32[1,1,256]{2,1,0:T(1,128)S(1)}, s32[1,1,256]{2,1,0:T(1,128)}, u32[]{:S(2)}) copy-start(s32[1,1,256]{2,1,0:T(1,128)} %param.23) | copy-start | bytes 3076
  2.2 0.7 %copy-start.4 = (f32[1,1,256]{2,1,0:T(1,128)S(1)}, f32[1,1,256]{2,1,0:T(1,128)}, u32[]{:S(2)}) copy-start(f32[1,1,256]{2,1,0:T(1,128)} %param.13) | copy-start | bytes 3076
where the time goes:
time: 49.2 us; the launch traced here: 48.8 us
  Pallas kernels  41.7 us (85%)
  local copies, waits for them, and re-layouts  6.36 us (13%)
  between operations  0.78 us (2%)
    pallas_call x1, Pallas kernels, on_device(): pl.pallas_call(functools.partial(kernel, dom, serve, steps, blocks), out_...  41.7 us
    unnamed x29, local copies, waits for them, and re-layouts  6.36 us

commit v1 on v0

v1 whole, which is shorter than its diff:
```python
import functools
import jax
import jax.numpy as jnp
from jax import lax
from jax.experimental import pallas as pl
from jax.experimental.pallas import tpu as pltpu
from jax.sharding import PartitionSpec as P

LEARN_RATE = 0.1
EPSILON = 1e-08
BLOCK = 128
CHUNK = 256
WIRE_MAX = 32767.0
TINY = 1e-30
MESH = pl.DeviceIdType.MESH
F32 = jnp.float32
BF16 = jnp.bfloat16


def dot(a, b, contract=((1,), (0,))):
    return lax.dot_general(a, b, (contract, ((), ())), preferred_element_type=F32)


def split(x):
    high = x.astype(BF16)
    return high, (x - high.astype(F32)).astype(BF16)


def to_wire(u):
    most = jnp.maximum(jnp.max(jnp.abs(u), axis=0, keepdims=True), TINY)
    return jnp.floor(u * (WIRE_MAX / most) + 0.5).astype(jnp.int32).astype(jnp.int16), most


def from_wire(q, most):
    return q.astype(jnp.int32).astype(F32) * (most * (1.0 / WIRE_MAX))


def adagrad(weights, state, grad):
    state = state + jnp.mean(grad * grad, axis=0, keepdims=True)
    rate = LEARN_RATE / (jnp.sqrt(state) + EPSILON)
    return weights - rate * grad, state


def kernel(
    dom, serve, steps, blocks,
    src, sst, tgt, tst, rel, sid, tid, rid, nb, cnt, shard, changed,
    o_src, o_sst, o_tgt, o_tst, o_served,
    ubuf, wire, mbuf, msend, code, code_in, pay, pay_in, expand,
    relg, qhi, qlo, whi, wlo,
    u_send, u_recv, m_send, m_recv, c_send, c_recv, p_send, p_recv,
):
    width, rows = src.shape
    nrel = rel.shape[0]
    chunks = blocks * BLOCK // CHUNK
    per = CHUNK // BLOCK
    slots = pay.shape[1]
    nt = ((1,), (1,))
    d = lax.axis_index("dom")
    s = lax.axis_index("serve")
    right, left = lax.rem(d + 1, dom), lax.rem(d + dom - 1, dom)
    peers = [lax.rem(s + j, serve) for j in range(1, serve)]

    barrier = pltpu.get_barrier_semaphore()
    for neighbour in (left, right):
        pl.semaphore_signal(barrier, inc=1, device_id=(neighbour, s), device_id_type=MESH)
    for peer in peers:
        pl.semaphore_signal(barrier, inc=1, device_id=(d, peer), device_id_type=MESH)

    eight = lax.broadcasted_iota(jnp.int32, (8, rows), 0)
    wire[0], most = to_wire(tgt[...])
    msend[0] = jnp.where(eight == 0, tst[...], most)
    code[...] = jnp.broadcast_to(
        jnp.where(changed[...] == 1, shard[...], -1).astype(F32), (8, rows)
    )
    pl.semaphore_wait(barrier, 2 + serve - 1)

    def ring(step):
        u = pltpu.make_async_remote_copy(
            src_ref=wire.at[step], dst_ref=ubuf.at[step], send_sem=u_send.at[step],
            recv_sem=u_recv.at[step], device_id=(right, s), device_id_type=MESH)
        m = pltpu.make_async_remote_copy(
            src_ref=msend.at[step], dst_ref=mbuf.at[step], send_sem=m_send.at[step],
            recv_sem=m_recv.at[step], device_id=(right, s), device_id_type=MESH)
        u.start()
        m.start()
        return u, m

    moving = ring(0)
    code_copies = []
    for j, peer in enumerate(peers):
        c = pltpu.make_async_remote_copy(
            src_ref=code, dst_ref=code_in.at[j], send_sem=c_send.at[j],
            recv_sem=c_recv.at[j], device_id=(d, peer), device_id_type=MESH)
        c.start()
        code_copies.append(c)

    row_of = lax.broadcasted_iota(jnp.int32, (rows, CHUNK), 0)
    edge = lax.broadcasted_iota(jnp.int32, (1, CHUNK), 1)

    def ids(ref, step, c):
        return jnp.concatenate(
            [ref[step, c * per + i : c * per + i + 1, :] for i in range(per)], axis=1)

    def one_hot(ref, step, c):
        return row_of == ids(ref, step, c)

    def ones(mask):
        return jnp.where(mask, 1.0, 0.0).astype(BF16)

    def per_edge(ref, step, c, offset):
        value = ref[step, c * per]
        for i in range(1, per):
            value = jnp.where(edge >= i * BLOCK, ref[step, c * per + i] + i * offset, value)
        return value

    parts, rest = [], rel[...]
    for i in range(3):
        parts.append(rest.astype(BF16).astype(F32))
        rest = rest - parts[-1]
    parts.append(jnp.zeros((BLOCK - 3 * nrel, width), F32))
    table = jnp.concatenate(parts, axis=0).T.astype(BF16)
    sub = lax.broadcasted_iota(jnp.int32, (BLOCK, CHUNK), 0)
    rel_of = jnp.where(sub < 3 * nrel, lax.rem(sub, nrel), -1)

    def relations(step):
        for c in range(chunks):
            at = (step * chunks + c) * CHUNK
            relg[:, at : at + CHUNK] = dot(table, ones(rel_of == ids(rid, step, c)))

    def queries(step, source):
        high, low = split(source)
        for c in range(chunks):
            hot = ones(one_hot(sid, step, c))
            at = (step * chunks + c) * CHUNK
            q = (dot(high, hot) + dot(low, hot)) * relg[:, at : at + CHUNK]
            q_high, q_low = split(q)
            qhi[:, c * CHUNK : (c + 1) * CHUNK] = q_high
            qlo[:, c * CHUNK : (c + 1) * CHUNK] = q_low

    def weights(step, target):
        high, low = split(target.T)
        for c in range(chunks):
            at = slice(c * CHUNK, (c + 1) * CHUNK)
            a, b = qhi[:, at], qlo[:, at]
            logits = dot(high, a) + dot(low, a) + dot(high, b)
            hot = one_hot(tid, step, c)
            valid = jnp.where(edge < per_edge(cnt, step, c, BLOCK), 1.0, 0.0)
            pos = jnp.sum(jnp.where(hot, logits, 0.0), axis=0, keepdims=True)
            dpos = -jax.nn.sigmoid(-pos) * valid
            negative = (row_of // BLOCK) == per_edge(nb, step, c, 0)
            dneg = jnp.where(negative, jax.nn.sigmoid(logits) * (valid / BLOCK), 0.0)
            w_high, w_low = split(jnp.where(hot, dpos, 0.0) + dneg)
            whi[:, at] = w_high
            wlo[:, at] = w_low

    def target_grad():
        total = jnp.zeros((width, rows), F32)
        for c in range(chunks):
            at = slice(c * CHUNK, (c + 1) * CHUNK)
            total += dot(qhi[:, at], whi[:, at], nt)
            total += dot(qlo[:, at], whi[:, at], nt)
            total += dot(qhi[:, at], wlo[:, at], nt)
        return total

    def source_grad(step, target):
        high, low = split(target)
        total = jnp.zeros((width, rows), F32)
        for c in range(chunks):
            at = slice(c * CHUNK, (c + 1) * CHUNK)
            g = dot(high, whi[:, at]) + dot(low, whi[:, at]) + dot(high, wlo[:, at])
            r = (step * chunks + c) * CHUNK
            g_high, g_low = split(g * relg[:, r : r + CHUNK])
            hot = ones(one_hot(sid, step, c))
            total += dot(g_high, hot, nt) + dot(g_low, hot, nt)
        return total

    def compaction(code_row, which):
        sel = jnp.where(code_row == which.astype(F32), 1.0, 0.0)
        before = lax.broadcasted_iota(jnp.int32, (rows, rows), 0)
        after = lax.broadcasted_iota(jnp.int32, (rows, rows), 1)
        rank = dot(jnp.broadcast_to(sel, (16, rows)).astype(BF16), ones(before < after))[:1, :]
        slot = lax.broadcasted_iota(jnp.int32, (slots, rows), 0).astype(F32)
        return ones((rank == slot) & (sel > 0.0))

    for step in range(steps):
        relations(step)
    source, source_state = src[...], sst[...]
    queries(0, source)
    for j in range(serve - 1):
        code_copies[j].wait()
        expand[j] = compaction(code_in[j, :1, :], s)

    target = None
    for step in range(steps):
        last = step == steps - 1
        for copy in moving:
            copy.wait()
        target = from_wire(ubuf[step], mbuf[step, 1:2, :])
        target_state = mbuf[step, :1, :]
        old = target
        weights(step, old)
        if not last:
            target, target_state = adagrad(target, target_state, target_grad())
            wire[step + 1], most = to_wire(target)
            msend[step + 1] = jnp.where(eight == 0, target_state, most)
            moving = ring(step + 1)
            source, source_state = adagrad(source, source_state, source_grad(step, old))
            queries(step + 1, source)
        else:
            source, source_state = adagrad(source, source_state, source_grad(step, old))
            published = source.astype(BF16)
            pay_copies = []
            for j, peer in enumerate(peers):
                pay[j] = dot(compaction(code[:1, :], peer), published, nt).astype(BF16)
                p = pltpu.make_async_remote_copy(
                    src_ref=pay.at[j], dst_ref=pay_in.at[j], send_sem=p_send.at[j],
                    recv_sem=p_recv.at[j], device_id=(d, peer), device_id_type=MESH)
                p.start()
                pay_copies.append(p)
            target, target_state = adagrad(target, target_state, target_grad())
            o_tgt[...] = target
            o_tst[...] = target_state
            o_src[...] = source
            o_sst[...] = source_state
            own = code[:1, :] == s.astype(F32)
            o_served[s] = jnp.where(own, source, 0.0).astype(BF16)
            for j in range(serve - 1):
                pay_copies[j].wait()
                sender = lax.rem(s + serve - 1 - j, serve)
                o_served[sender] = dot(pay_in[j], expand[j], ((0,), (0,))).astype(BF16)


def on_device(
    dom, serve,
    source_rows, source_state, target_rows, target_state, relation_table,
    source_ids, target_ids, relation_ids, negative_block, edge_counts,
    serving_shard, changed_rows,
):
    _, _, rows, width = source_rows.shape
    _, _, steps, blocks, _ = source_ids.shape
    nrel = relation_table.shape[0]
    slots = rows // 4
    edges = blocks * BLOCK
    vmem = pl.BlockSpec(memory_space=pltpu.VMEM)
    smem = pl.BlockSpec(memory_space=pltpu.SMEM)
    dma = pltpu.SemaphoreType.DMA
    outs = pl.pallas_call(
        functools.partial(kernel, dom, serve, steps, blocks),
        out_shape=(
            jax.ShapeDtypeStruct((width, rows), F32),
            jax.ShapeDtypeStruct((1, rows), F32),
            jax.ShapeDtypeStruct((width, rows), F32),
            jax.ShapeDtypeStruct((1, rows), F32),
            jax.ShapeDtypeStruct((serve, width, rows), BF16),
        ),
        in_specs=[vmem] * 8 + [smem] * 2 + [vmem] * 2,
        out_specs=(vmem,) * 5,
        scratch_shapes=[
            pltpu.VMEM((steps, width, rows), jnp.int16),
            pltpu.VMEM((steps, width, rows), jnp.int16),
            pltpu.VMEM((steps, 8, rows), F32),
            pltpu.VMEM((steps, 8, rows), F32),
            pltpu.VMEM((8, rows), F32),
            pltpu.VMEM((serve - 1, 8, rows), F32),
            pltpu.VMEM((serve - 1, slots, width), BF16),
            pltpu.VMEM((serve - 1, slots, width), BF16),
            pltpu.VMEM((serve - 1, slots, rows), BF16),
            pltpu.VMEM((width, steps * edges), F32),
            pltpu.VMEM((width, edges), BF16),
            pltpu.VMEM((width, edges), BF16),
            pltpu.VMEM((rows, edges), BF16),
            pltpu.VMEM((rows, edges), BF16),
            dma((steps,)), dma((steps,)), dma((steps,)), dma((steps,)),
            dma((serve - 1,)), dma((serve - 1,)), dma((serve - 1,)), dma((serve - 1,)),
        ],
        compiler_params=pltpu.CompilerParams(
            collective_id=0, has_side_effects=True, vmem_limit_bytes=48 * 1024 * 1024
        ),
        name="train_and_publish",
    )(
        source_rows[0, 0].T, source_state[0], target_rows[0, 0].T, target_state[0],
        relation_table, source_ids[0, 0], target_ids[0, 0], relation_ids[0, 0],
        negative_block[0, 0], edge_counts[0, 0], serving_shard[0], changed_rows[0],
    )
    source, source_sums, target, target_sums, served = outs
    return (source.T[None, None], source_sums[None], target.T[None, None], target_sums[None],
            jnp.swapaxes(served, 1, 2)[None, None])


def solution(mesh):
    rows4 = P("dom", "serve", None, None)
    rows3 = P("dom", "serve", None)
    ids = P("dom", "serve", None, None, None)
    return jax.shard_map(
        functools.partial(on_device, mesh.shape["dom"], mesh.shape["serve"]),
        mesh=mesh,
        in_specs=(rows4, rows3, rows4, rows3, P(), ids, ids, ids, rows4, rows4, rows3, rows3),
        out_specs=(rows4, rows3, rows4, rows3, ids),
        check_vma=False,
    )
```

time: 49.2 us -> 38.8 us (0.79)
  Pallas kernels: 41.7 us -> 28.4 us
  local copies, waits for them, and re-layouts: 6.36 us -> 9.05 us
    pallas_call x1, Pallas kernels: 41.7 us -> 28.4 us  [on_device(): pl.pallas_call(functools.partial(kernel, dom, serve, steps, blocks), out_...]
    unnamed x29, local copies, waits for them, and re-layouts: 6.36 us -> 9.05 us
where the time goes in v1:
time: 38.8 us; the launch traced here: 38.2 us
  Pallas kernels  28.4 us (73%)
  local copies, waits for them, and re-layouts  9.05 us (23%)
  between operations  0.7 us (2%)
    pallas_call x1, Pallas kernels, on_device(): pl.pallas_call(functools.partial(kernel, dom, serve, steps, blocks), out_...  28.4 us
    unnamed x29, local copies, waits for them, and re-layouts  9.05 us

profile of v1, /device:TPU:1, one launch (start us, length us, event | category | flops | bytes accessed | tf_op | source)
XLA Modules:
  0.0 38.2 jit_solution(3628198567557534417)
XLA Ops:
  0.6 0.0 copy-start.8
  0.6 0.0 copy-start.9
  0.7 0.0 copy-start.7
  0.7 0.0 copy-start.4
  0.7 0.0 copy-start.3
  0.7 0.0 copy-start.6
  0.7 0.6 %copy-done.8 = s32[1,1,2,8]{3,2,1,0:T(2,128)S(1)} copy-done((s32[1,1,2,8]{3,2,1,0:T(2,128)S(1)}, s32[1,1,2,8]{3,2,1,0:T(2,128)}, u32[]{:S(2)}) %copy-start.8) | copy-done | bytes 88
  1.3 0.0 copy-done.9
  1.3 0.0 copy-done.7
  1.3 0.0 copy-done.4
  1.4 0.0 copy-done.3
  1.4 0.0 copy-done.6
  1.4 0.0 copy-start
  1.4 1.0 %copy-done = f32[1,1,256,400]{2,3,1,0:T(8,128)S(1)} copy-done((f32[1,1,256,400]{2,3,1,0:T(8,128)S(1)}, f32[1,1,256,400]{2,3,1,0:T(8,128)}, u32[]{:S(2)}) %copy-start) | copy-done | bytes 409624
  2.4 0.0 copy-start.1
  2.4 1.0 %copy-done.1 = f32[1,1,256,400]{2,3,1,0:T(8,128)S(1)} copy-done((f32[1,1,256,400]{2,3,1,0:T(8,128)S(1)}, f32[1,1,256,400]{2,3,1,0:T(8,128)}, u32[]{:S(2)}) %copy-start.1) | copy-done | bytes 409624
  3.4 0.0 copy-start.2
  3.4 0.8 %copy-done.2 = f32[16,400]{1,0:T(8,128)S(1)} copy-done((f32[16,400]{1,0:T(8,128)S(1)}, f32[16,400]{1,0:T(8,128)}, u32[]{:S(2)}) %copy-start.2) | copy-done | bytes 25624
  4.2 0.0 copy-start.5
  4.2 0.7 %copy-done.5 = s32[1,1,2,8,128]{4,3,2,1,0:T(8,128)S(1)} copy-done((s32[1,1,2,8,128]{4,3,2,1,0:T(8,128)S(1)}, s32[1,1,2,8,128]{4,3,2,1,0:T(8,128)}, u32[]{:S(2)}) %copy-start.5) | copy-done | bytes 8216
  4.9 0.0 copy-start.10
  4.9 0.7 %copy-done.10 = s32[1,1,256]{2,1,0:T(1,128)S(1)} copy-done((s32[1,1,256]{2,1,0:T(1,128)S(1)}, s32[1,1,256]{2,1,0:T(1,128)}, u32[]{:S(2)}) %copy-start.10) | copy-done | bytes 1048
  5.5 0.0 copy-start.11
  5.5 0.7 %copy-done.11 = s32[1,1,256]{2,1,0:T(1,128)S(1)} copy-done((s32[1,1,256]{2,1,0:T(1,128)S(1)}, s32[1,1,256]{2,1,0:T(1,128)}, u32[]{:S(2)}) %copy-start.11) | copy-done | bytes 1048
  6.2 28.4 %train_and_publish.1 = (f32[400,256]{1,0:T(8,128)S(1)}, f32[1,256]{1,0:T(1,128)S(1)}, f32[400,256]{1,0:T(8,128)S(1)}, f32[1,256]{1,0:T(1,128)S(1)}, bf16[4,400,256]{2,1,0:T(8,128)(2,1)S(1)}) custom-call(f32[400,256]{1,0:T(8,128)S(1)} %bitcast.27, f32[1,256]{1,0:T(1,128)S(1)} %bitcast.34, f32[400,256]{1,0:T(8,128)S(1)} %bitcast.28, f32[1,256]{1,0:T(1,128)S(1)} %bitcast.35, ...), custom_call_target="tpu_custom_call" | custom-call | tf_op jit(solution)/shard_map/train_and_publish/pallas_call | solution.py:247
  34.6 0.8 %copy.22 = f32[1,1,256,400]{2,3,1,0:T(8,128)} copy(f32[1,1,256,400]{2,3,1,0:T(8,128)S(1)} %bitcast.30) | data formatting | bytes 819200
  35.4 0.6 %copy.23 = f32[1,1,256]{2,1,0:T(1,128)} copy(f32[1,1,256]{2,1,0:T(1,128)S(1)} %bitcast.41) | data formatting | bytes 2048
  36.0 0.8 %copy.24 = f32[1,1,256,400]{2,3,1,0:T(8,128)} copy(f32[1,1,256,400]{2,3,1,0:T(8,128)S(1)} %bitcast.29) | data formatting | bytes 819200
  36.7 0.6 %copy.25 = f32[1,1,256]{2,1,0:T(1,128)} copy(f32[1,1,256]{2,1,0:T(1,128)S(1)} %bitcast.40) | data formatting | bytes 2048
  37.3 0.9 %copy.26 = bf16[1,1,4,256,400]{3,4,2,1,0:T(8,128)(2,1)} copy(bf16[1,1,4,256,400]{3,4,2,1,0:T(8,128)(2,1)S(1)} %bitcast.26) | data formatting | bytes 1638400
Async XLA Ops:
  0.6 0.7 %copy-start.8 = (s32[1,1,2,8]{3,2,1,0:T(2,128)S(1)}, s32[1,1,2,8]{3,2,1,0:T(2,128)}, u32[]{:S(2)}) copy-start(s32[1,1,2,8]{3,2,1,0:T(2,128)} %param.20) | copy-start | bytes 196
  0.6 0.7 %copy-start.9 = (s32[1,1,2,8]{3,2,1,0:T(2,128)S(1)}, s32[1,1,2,8]{3,2,1,0:T(2,128)}, u32[]{:S(2)}) copy-start(s32[1,1,2,8]{3,2,1,0:T(2,128)} %param.21) | copy-start | bytes 196
  0.7 0.7 %copy-start.7 = (f32[1,1,256]{2,1,0:T(1,128)S(1)}, f32[1,1,256]{2,1,0:T(1,128)}, u32[]{:S(2)}) copy-start(f32[1,1,256]{2,1,0:T(1,128)} %param.15) | copy-start | bytes 3076
  0.7 0.7 %copy-start.4 = (s32[1,1,2,8,128]{4,3,2,1,0:T(8,128)S(1)}, s32[1,1,2,8,128]{4,3,2,1,0:T(8,128)}, u32[]{:S(2)}) copy-start(s32[1,1,2,8,128]{4,3,2,1,0:T(8,128)} %param.18) | copy-start | bytes 24580
  0.7 0.7 %copy-start.3 = (s32[1,1,2,8,128]{4,3,2,1,0:T(8,128)S(1)}, s32[1,1,2,8,128]{4,3,2,1,0:T(8,128)}, u32[]{:S(2)}) copy-start(s32[1,1,2,8,128]{4,3,2,1,0:T(8,128)} %param.17) | copy-start | bytes 24580
  0.7 0.7 %copy-start.6 = (f32[1,1,256]{2,1,0:T(1,128)S(1)}, f32[1,1,256]{2,1,0:T(1,128)}, u32[]{:S(2)}) copy-start(f32[1,1,256]{2,1,0:T(1,128)} %param.13) | copy-start | bytes 3076
  1.4 1.0 %copy-start = (f32[1,1,256,400]{2,3,1,0:T(8,128)S(1)}, f32[1,1,256,400]{2,3,1,0:T(8,128)}, u32[]{:S(2)}) copy-start(f32[1,1,256,400]{2,3,1,0:T(8,128)} %param.12) | copy-start | bytes 1228804
  2.4 1.0 %copy-start.1 = (f32[1,1,256,400]{2,3,1,0:T(8,128)S(1)}, f32[1,1,256,400]{2,3,1,0:T(8,128)}, u32[]{:S(2)}) copy-start(f32[1,1,256,400]{2,3,1,0:T(8,128)} %param.14) | copy-start | bytes 1228804
  3.4 0.8 %copy-start.2 = (f32[16,400]{1,0:T(8,128)S(1)}, f32[16,400]{1,0:T(8,128)}, u32[]{:S(2)}) copy-start(f32[16,400]{1,0:T(8,128)} %rel.1) | copy-start | bytes 76804
  4.2 0.7 %copy-start.5 = (s32[1,1,2,8,128]{4,3,2,1,0:T(8,128)S(1)}, s32[1,1,2,8,128]{4,3,2,1,0:T(8,128)}, u32[]{:S(2)}) copy-start(s32[1,1,2,8,128]{4,3,2,1,0:T(8,128)} %param.19) | copy-start | bytes 24580
  4.9 0.7 %copy-start.10 = (s32[1,1,256]{2,1,0:T(1,128)S(1)}, s32[1,1,256]{2,1,0:T(1,128)}, u32[]{:S(2)}) copy-start(s32[1,1,256]{2,1,0:T(1,128)} %param.22) | copy-start | bytes 3076
  5.5 0.7 %copy-start.11 = (s32[1,1,256]{2,1,0:T(1,128)S(1)}, s32[1,1,256]{2,1,0:T(1,128)}, u32[]{:S(2)}) copy-start(s32[1,1,256]{2,1,0:T(1,128)} %param.23) | copy-start | bytes 3076

commit v2 on v1

--- a/solution.py
+++ b/solution.py
@@ -43,11 +43,14 @@
 
 def kernel(
     dom, serve, steps, blocks,
+    src_in, sst_in, tgt_in, tst_in, rel_in, sid_in, tid_in, rid_in, nb_in, cnt_in, shard_in,
+    changed_in,
+    o_src, o_sst, o_tgt, o_tst, o_pay, o_expand, o_code,
+    new_src, new_sst, new_tgt, new_tst, expand, own,
     src, sst, tgt, tst, rel, sid, tid, rid, nb, cnt, shard, changed,
-    o_src, o_sst, o_tgt, o_tst, o_served,
-    ubuf, wire, mbuf, msend, code, code_in, pay, pay_in, expand,
+    ubuf, wire, mbuf, msend, code, code_in, pay, pay_in, pick,
     relg, qhi, qlo, whi, wlo,
-    u_send, u_recv, m_send, m_recv, c_send, c_recv, p_send, p_recv,
+    loaded, stored, u_send, u_recv, m_send, m_recv, c_send, c_recv, p_send, p_recv,
 ):
     width, rows = src.shape
     nrel = rel.shape[0]
@@ -60,6 +63,20 @@
     right, left = lax.rem(d + 1, dom), lax.rem(d + dom - 1, dom)
     peers = [lax.rem(s + j, serve) for j in range(1, serve)]
 
+    loads = {}
+    for i, (name, given, held) in enumerate((
+        ("tgt", tgt_in, tgt), ("tst", tst_in, tst), ("shard", shard_in, shard),
+        ("changed", changed_in, changed), ("rel", rel_in, rel), ("rid", rid_in, rid),
+        ("src", src_in, src), ("sid", sid_in, sid), ("sst", sst_in, sst), ("tid", tid_in, tid),
+        ("nb", nb_in, nb), ("cnt", cnt_in, cnt),
+    )):
+        loads[name] = pltpu.make_async_copy(given, held, loaded.at[i])
+        loads[name].start()
+
+    def arrived(*names):
+        for name in names:
+            loads[name].wait()
+
     barrier = pltpu.get_barrier_semaphore()
     for neighbour in (left, right):
         pl.semaphore_signal(barrier, inc=1, device_id=(neighbour, s), device_id_type=MESH)
@@ -67,8 +84,10 @@
         pl.semaphore_signal(barrier, inc=1, device_id=(d, peer), device_id_type=MESH)
 
     eight = lax.broadcasted_iota(jnp.int32, (8, rows), 0)
+    arrived("tgt", "tst")
     wire[0], most = to_wire(tgt[...])
     msend[0] = jnp.where(eight == 0, tst[...], most)
+    arrived("shard", "changed")
     code[...] = jnp.broadcast_to(
         jnp.where(changed[...] == 1, shard[...], -1).astype(F32), (8, rows)
     )
@@ -108,11 +127,13 @@
         return jnp.where(mask, 1.0, 0.0).astype(BF16)
 
     def per_edge(ref, step, c, offset):
-        value = ref[step, c * per]
-        for i in range(1, per):
-            value = jnp.where(edge >= i * BLOCK, ref[step, c * per + i] + i * offset, value)
-        return value
-
+        return jnp.concatenate([
+            jnp.broadcast_to(ref[step : step + 1, c * per + i : c * per + i + 1], (1, BLOCK))
+            + i * offset
+            for i in range(per)
+        ], axis=1)
+
+    arrived("rel", "rid")
     parts, rest = [], rel[...]
     for i in range(3):
         parts.append(rest.astype(BF16).astype(F32))
@@ -184,12 +205,27 @@
 
     for step in range(steps):
         relations(step)
-    source, source_state = src[...], sst[...]
+    arrived("src", "sid")
+    source = src[...]
     queries(0, source)
+    arrived("sst", "tid", "nb", "cnt")
+    source_state = sst[...]
+    own[...] = jnp.where(code[:1, :] == s.astype(F32), 1.0, 0.0)
+    for j, peer in enumerate(peers):
+        pick[j] = compaction(code[:1, :], peer)
     for j in range(serve - 1):
         code_copies[j].wait()
         expand[j] = compaction(code_in[j, :1, :], s)
 
+    stores = []
+
+    def store(*pairs):
+        for held, out in pairs:
+            copy = pltpu.make_async_copy(held, out, stored.at[len(stores)])
+            copy.start()
+            stores.append(copy)
+
+    store((expand, o_expand), (own, o_code))
     target = None
     for step in range(steps):
         last = step == steps - 1
@@ -211,23 +247,58 @@
             published = source.astype(BF16)
             pay_copies = []
             for j, peer in enumerate(peers):
-                pay[j] = dot(compaction(code[:1, :], peer), published, nt).astype(BF16)
+                pay[j] = dot(pick[j], published, nt).astype(BF16)
                 p = pltpu.make_async_remote_copy(
                     src_ref=pay.at[j], dst_ref=pay_in.at[j], send_sem=p_send.at[j],
                     recv_sem=p_recv.at[j], device_id=(d, peer), device_id_type=MESH)
                 p.start()
                 pay_copies.append(p)
+            new_src[...] = source
+            new_sst[...] = source_state
+            store((new_src, o_src), (new_sst, o_sst))
             target, target_state = adagrad(target, target_state, target_grad())
-            o_tgt[...] = target
-            o_tst[...] = target_state
-            o_src[...] = source
-            o_sst[...] = source_state
-            own = code[:1, :] == s.astype(F32)
-            o_served[s] = jnp.where(own, source, 0.0).astype(BF16)
+            new_tgt[...] = target
+            new_tst[...] = target_state
+            store((new_tgt, o_tgt), (new_tst, o_tst))
             for j in range(serve - 1):
                 pay_copies[j].wait()
-                sender = lax.rem(s + serve - 1 - j, serve)
-                o_served[sender] = dot(pay_in[j], expand[j], ((0,), (0,))).astype(BF16)
+            store((pay_in, o_pay))
+            for copy in stores:
+                copy.wait()
+
+
+def finish(serve, src, sst, tgt, tst, pay_in, expand_in, own_in, *refs):
+    (o_src, o_sst, o_tgt, o_tst, o_served,
+     served, source, pay, expand, own, loaded, stored, served_sems) = refs
+    loads = [
+        pltpu.make_async_copy(given, held, loaded.at[i])
+        for i, (given, held) in enumerate(
+            ((pay_in, pay), (expand_in, expand), (src, source), (own_in, own)))
+    ]
+    copies = [
+        pltpu.make_async_copy(given, out, stored.at[i])
+        for i, (given, out) in enumerate(
+            ((src, o_src), (tgt, o_tgt), (sst, o_sst), (tst, o_tst)))
+    ]
+    for copy in loads + copies:
+        copy.start()
+    s = lax.axis_index("serve")
+    for load in loads[:2]:
+        load.wait()
+    for j in range(1, serve + 1):
+        if j == serve:
+            for load in loads[2:]:
+                load.wait()
+            piece = jnp.where(own[...] > 0.0, source[...], 0.0)
+        else:
+            piece = dot(pay[j - 1], expand[j - 1], ((0,), (0,)))
+        served[j - 1] = piece.astype(BF16)
+        sender = lax.rem(s + serve - j, serve)
+        copy = pltpu.make_async_copy(served.at[j - 1], o_served.at[sender], served_sems.at[j - 1])
+        copy.start()
+        copies.append(copy)
+    for copy in copies:
+        copy.wait()
 
 
 def on_device(
@@ -241,21 +312,32 @@
     nrel = relation_table.shape[0]
     slots = rows // 4
     edges = blocks * BLOCK
-    vmem = pl.BlockSpec(memory_space=pltpu.VMEM)
-    smem = pl.BlockSpec(memory_space=pltpu.SMEM)
+    hbm = pl.BlockSpec(memory_space=pltpu.HBM)
     dma = pltpu.SemaphoreType.DMA
+    args = (
+        source_rows[0, 0].T, source_state[0], target_rows[0, 0].T, target_state[0],
+        relation_table, source_ids[0, 0], target_ids[0, 0], relation_ids[0, 0],
+        negative_block[0, 0], edge_counts[0, 0], serving_shard[0], changed_rows[0],
+    )
+    state = (
+        jax.ShapeDtypeStruct((width, rows), F32),
+        jax.ShapeDtypeStruct((1, rows), F32),
+        jax.ShapeDtypeStruct((width, rows), F32),
+        jax.ShapeDtypeStruct((1, rows), F32),
+    )
+    handed = state + (
+        jax.ShapeDtypeStruct((serve - 1, slots, width), BF16),
+        jax.ShapeDtypeStruct((serve - 1, slots, rows), BF16),
+        jax.ShapeDtypeStruct((1, rows), F32),
+    )
     outs = pl.pallas_call(
         functools.partial(kernel, dom, serve, steps, blocks),
-        out_shape=(
-            jax.ShapeDtypeStruct((width, rows), F32),
-            jax.ShapeDtypeStruct((1, rows), F32),
-            jax.ShapeDtypeStruct((width, rows), F32),
-            jax.ShapeDtypeStruct((1, rows), F32),
-            jax.ShapeDtypeStruct((serve, width, rows), BF16),
-        ),
-        in_specs=[vmem] * 8 + [smem] * 2 + [vmem] * 2,
-        out_specs=(vmem,) * 5,
+        out_shape=handed,
+        in_specs=[hbm] * len(args),
+        out_specs=(hbm,) * len(handed),
         scratch_shapes=[
+            pltpu.VMEM(held.shape, held.dtype) for held in state + handed[5:] + args
+        ] + [
             pltpu.VMEM((steps, width, rows), jnp.int16),
             pltpu.VMEM((steps, width, rows), jnp.int16),
             pltpu.VMEM((steps, 8, rows), F32),
@@ -270,19 +352,31 @@
             pltpu.VMEM((width, edges), BF16),
             pltpu.VMEM((rows, edges), BF16),
             pltpu.VMEM((rows, edges), BF16),
+            dma((len(args),)), dma((len(handed),)),
             dma((steps,)), dma((steps,)), dma((steps,)), dma((steps,)),
             dma((serve - 1,)), dma((serve - 1,)), dma((serve - 1,)), dma((serve - 1,)),
         ],
         compiler_params=pltpu.CompilerParams(
-            collective_id=0, has_side_effects=True, vmem_limit_bytes=48 * 1024 * 1024
+            collective_id=0, has_side_effects=True, vmem_limit_bytes=60 * 1024 * 1024
         ),
-        name="train_and_publish",
-    )(
-        source_rows[0, 0].T, source_state[0], target_rows[0, 0].T, target_state[0],
-        relation_table, source_ids[0, 0], target_ids[0, 0], relation_ids[0, 0],
-        negative_block[0, 0], edge_counts[0, 0], serving_shard[0], changed_rows[0],
-    )
-    source, source_sums, target, target_sums, served = outs
+        name="train",
+    )(*args)
+    source, source_sums, target, target_sums, served = pl.pallas_call(
+        functools.partial(finish, serve),
+        out_shape=state + (jax.ShapeDtypeStruct((serve, width, rows), BF16),),
+        in_specs=[hbm] * len(handed),
+        out_specs=(hbm,) * 5,
+        scratch_shapes=[
+            pltpu.VMEM((serve, width, rows), BF16),
+            pltpu.VMEM((width, rows), F32),
+            pltpu.VMEM(handed[4].shape, BF16),
+            pltpu.VMEM(handed[5].shape, BF16),
+            pltpu.VMEM((1, rows), F32),
+            dma((4,)), dma((4,)), dma((serve,)),
+        ],
+        compiler_params=pltpu.CompilerParams(vmem_limit_bytes=60 * 1024 * 1024),
+        name="publish",
+    )(*outs)
     return (source.T[None, None], source_sums[None], target.T[None, None], target_sums[None],
             jnp.swapaxes(served, 1, 2)[None, None])
 

time: 38.8 us -> 55.1 us (1.42)
  Pallas kernels: 28.4 us -> 54.3 us
  local copies, waits for them, and re-layouts: 9.05 us -> 0 us
    pallas_call x0 -> x1, Pallas kernels: none -> 26.1 us  [on_device(): pl.pallas_call(functools.partial(finish, serve), out_shape=state + (jax.S...]
    unnamed x29 -> x0, local copies, waits for them, and re-layouts: 9.05 us -> none
where the time goes in v2:
time: 55.1 us; the launch traced here: 54.9 us
  Pallas kernels  54.3 us (99%)
  between operations  0.64 us (1%)
    pallas_call x1, Pallas kernels, on_device(): pl.pallas_call(functools.partial(kernel, dom, serve, steps, blocks), out_...  28.2 us
    pallas_call x1, Pallas kernels, on_device(): pl.pallas_call(functools.partial(finish, serve), out_shape=state + (jax.S...  26.1 us

profile of v2, /device:TPU:1, one launch (start us, length us, event | category | flops | bytes accessed | tf_op | source)
XLA Modules:
  0.0 54.9 jit_solution(18237576973726570421)
XLA Ops:
  0.6 28.2 %train.1 = (f32[400,256]{1,0:T(8,128)}, f32[1,256]{1,0:T(1,128)}, f32[400,256]{1,0:T(8,128)}, f32[1,256]{1,0:T(1,128)}, bf16[3,64,400]{2,1,0:T(8,128)(2,1)}, /*i...) custom-call(f32[400,256]{1,0:T(8,128)} %bitcast.26, f32[1,256]{1,0:T(1,128)} %bitcast.31, f32[400,256]{1,0:T(8,128)} %bitcast.27, ...), custom_call_target="tpu_custom_call" | custom-call | tf_op jit(solution)/shard_map/train/pallas_call | solution.py:333
  28.8 26.1 %publish.1 = (f32[400,256]{1,0:T(8,128)}, f32[1,256]{1,0:T(1,128)}, f32[400,256]{1,0:T(8,128)}, f32[1,256]{1,0:T(1,128)}, bf16[4,400,256]{2,1,0:T(8,128)(2,1)}) custom-call(f32[400,256]{1,0:T(8,128)} %get-tuple-element.17.src, f32[1,256]{1,0:T(1,128)} %get-tuple-element.18.sst, f32[400,256]{1,0:T(8,128)} %get-tuple-element.19.tgt, ...), custom_call_target="tpu_custom_call" | custom-call | tf_op jit(solution)/shard_map/publish/pallas_call | solution.py:364

commit v3 on v2

--- a/solution.py
+++ b/solution.py
@@ -267,36 +267,35 @@
                 copy.wait()
 
 
-def finish(serve, src, sst, tgt, tst, pay_in, expand_in, own_in, *refs):
-    (o_src, o_sst, o_tgt, o_tst, o_served,
-     served, source, pay, expand, own, loaded, stored, served_sems) = refs
-    loads = [
-        pltpu.make_async_copy(given, held, loaded.at[i])
-        for i, (given, held) in enumerate(
-            ((pay_in, pay), (expand_in, expand), (src, source), (own_in, own)))
-    ]
-    copies = [
-        pltpu.make_async_copy(given, out, stored.at[i])
-        for i, (given, out) in enumerate(
-            ((src, o_src), (tgt, o_tgt), (sst, o_sst), (tst, o_tst)))
-    ]
-    for copy in loads + copies:
-        copy.start()
+def finish(serve, *refs):
+    given, outs, held = refs[:7], refs[7:11], refs[12:19]
+    o_served, served, loaded, stored, served_sems = refs[11], *refs[19:]
+    src, _, _, _, pay, expand, own = held
+    order = (4, 5, 0, 6, 2, 1, 3)
+    loads = {i: pltpu.make_async_copy(given[i], held[i], loaded.at[i]) for i in order}
+    for i in order:
+        loads[i].start()
+    copies = []
+
+    def store(value, out, sem):
+        copies.append(pltpu.make_async_copy(value, out, sem))
+        copies[-1].start()
+
     s = lax.axis_index("serve")
-    for load in loads[:2]:
-        load.wait()
+    loads[4].wait()
+    loads[5].wait()
     for j in range(1, serve + 1):
         if j == serve:
-            for load in loads[2:]:
-                load.wait()
-            piece = jnp.where(own[...] > 0.0, source[...], 0.0)
+            for i in order[2:]:
+                loads[i].wait()
+                if i < 4:
+                    store(held[i], outs[i], stored.at[i])
+            piece = jnp.where(own[...] > 0.0, src[...], 0.0)
         else:
             piece = dot(pay[j - 1], expand[j - 1], ((0,), (0,)))
         served[j - 1] = piece.astype(BF16)
         sender = lax.rem(s + serve - j, serve)
-        copy = pltpu.make_async_copy(served.at[j - 1], o_served.at[sender], served_sems.at[j - 1])
-        copy.start()
-        copies.append(copy)
+        store(served.at[j - 1], o_served.at[sender], served_sems.at[j - 1])
     for copy in copies:
         copy.wait()
 
@@ -366,13 +365,9 @@
         out_shape=state + (jax.ShapeDtypeStruct((serve, width, rows), BF16),),
         in_specs=[hbm] * len(handed),
         out_specs=(hbm,) * 5,
-        scratch_shapes=[
+        scratch_shapes=[pltpu.VMEM(held.shape, held.dtype) for held in handed] + [
             pltpu.VMEM((serve, width, rows), BF16),
-            pltpu.VMEM((width, rows), F32),
-            pltpu.VMEM(handed[4].shape, BF16),
-            pltpu.VMEM(handed[5].shape, BF16),
-            pltpu.VMEM((1, rows), F32),
-            dma((4,)), dma((4,)), dma((serve,)),
+            dma((len(handed),)), dma((4,)), dma((serve,)),
         ],
         compiler_params=pltpu.CompilerParams(vmem_limit_bytes=60 * 1024 * 1024),
         name="publish",

time: 55.1 us -> 31.6 us (0.57)
  Pallas kernels: 54.3 us -> 30.8 us
    pallas_call x1, Pallas kernels: 26.1 us -> 2.57 us  [on_device(): pl.pallas_call(functools.partial(finish, serve), out_shape=state + (jax.S...]
where the time goes in v3:
time: 31.6 us; the launch traced here: 31.4 us
  Pallas kernels  30.8 us (97%)
  between operations  0.64 us (2%)
    pallas_call x1, Pallas kernels, on_device(): pl.pallas_call(functools.partial(kernel, dom, serve, steps, blocks), out_...  28.2 us
    pallas_call x1, Pallas kernels, on_device(): pl.pallas_call(functools.partial(finish, serve), out_shape=state + (jax.S...  2.57 us

profile of v3, /device:TPU:1, one launch (start us, length us, event | category | flops | bytes accessed | tf_op | source)
XLA Modules:
  0.0 31.4 jit_solution(6902333060423416028)
XLA Ops:
  0.6 28.2 %train.1 = (f32[400,256]{1,0:T(8,128)}, f32[1,256]{1,0:T(1,128)}, f32[400,256]{1,0:T(8,128)}, f32[1,256]{1,0:T(1,128)}, bf16[3,64,400]{2,1,0:T(8,128)(2,1)}, /*i...) custom-call(f32[400,256]{1,0:T(8,128)} %bitcast.26, f32[1,256]{1,0:T(1,128)} %bitcast.31, f32[400,256]{1,0:T(8,128)} %bitcast.27, ...), custom_call_target="tpu_custom_call" | custom-call | tf_op jit(solution)/shard_map/train/pallas_call | solution.py:332
  28.8 2.6 %publish.1 = (f32[400,256]{1,0:T(8,128)}, f32[1,256]{1,0:T(1,128)}, f32[400,256]{1,0:T(8,128)}, f32[1,256]{1,0:T(1,128)}, bf16[4,400,256]{2,1,0:T(8,128)(2,1)}) custom-call(f32[400,256]{1,0:T(8,128)} %get-tuple-element.17.refs_0_, f32[1,256]{1,0:T(1,128)} %get-tuple-element.18.refs_1_, f32[400,256]{1,0:T(8,128)} %get-tuple-element.19.refs_2_, ...), custom_call_target="tpu_custom_call" | custom-call | tf_op jit(solution)/shard_map/publish/pallas_call | solution.py:363

commit v4 on v3

--- a/solution.py
+++ b/solution.py
@@ -83,28 +83,36 @@
     for peer in peers:
         pl.semaphore_signal(barrier, inc=1, device_id=(d, peer), device_id_type=MESH)
 
-    eight = lax.broadcasted_iota(jnp.int32, (8, rows), 0)
+    eight = lax.broadcasted_iota(jnp.int32, (8, BLOCK), 0)
+    halves = rows // BLOCK
+
+    def pack(step, h, target, state):
+        wire[step, h], most = to_wire(target)
+        msend[step, h] = jnp.where(eight == 0, state, most)
+
     arrived("tgt", "tst")
-    wire[0], most = to_wire(tgt[...])
-    msend[0] = jnp.where(eight == 0, tst[...], most)
+    for h in range(halves):
+        at = slice(h * BLOCK, (h + 1) * BLOCK)
+        pack(0, h, tgt[:, at], tst[:, at])
     arrived("shard", "changed")
     code[...] = jnp.broadcast_to(
         jnp.where(changed[...] == 1, shard[...], -1).astype(F32), (8, rows)
     )
     pl.semaphore_wait(barrier, 2 + serve - 1)
 
-    def ring(step):
+    def ring(step, h):
+        i = step * halves + h
         u = pltpu.make_async_remote_copy(
-            src_ref=wire.at[step], dst_ref=ubuf.at[step], send_sem=u_send.at[step],
-            recv_sem=u_recv.at[step], device_id=(right, s), device_id_type=MESH)
+            src_ref=wire.at[step, h], dst_ref=ubuf.at[step, h], send_sem=u_send.at[i],
+            recv_sem=u_recv.at[i], device_id=(right, s), device_id_type=MESH)
         m = pltpu.make_async_remote_copy(
-            src_ref=msend.at[step], dst_ref=mbuf.at[step], send_sem=m_send.at[step],
-            recv_sem=m_recv.at[step], device_id=(right, s), device_id_type=MESH)
+            src_ref=msend.at[step, h], dst_ref=mbuf.at[step, h], send_sem=m_send.at[i],
+            recv_sem=m_recv.at[i], device_id=(right, s), device_id_type=MESH)
         u.start()
         m.start()
         return u, m
 
-    moving = ring(0)
+    moving = [ring(0, h) for h in range(halves)]
     code_copies = []
     for j, peer in enumerate(peers):
         c = pltpu.make_async_remote_copy(
@@ -158,29 +166,29 @@
             qhi[:, c * CHUNK : (c + 1) * CHUNK] = q_high
             qlo[:, c * CHUNK : (c + 1) * CHUNK] = q_low
 
-    def weights(step, target):
+    def weights(step, h, target):
         high, low = split(target.T)
         for c in range(chunks):
             at = slice(c * CHUNK, (c + 1) * CHUNK)
             a, b = qhi[:, at], qlo[:, at]
             logits = dot(high, a) + dot(low, a) + dot(high, b)
-            hot = one_hot(tid, step, c)
+            hot = row_of[:BLOCK] == ids(tid, step, c) - h * BLOCK
             valid = jnp.where(edge < per_edge(cnt, step, c, BLOCK), 1.0, 0.0)
             pos = jnp.sum(jnp.where(hot, logits, 0.0), axis=0, keepdims=True)
             dpos = -jax.nn.sigmoid(-pos) * valid
-            negative = (row_of // BLOCK) == per_edge(nb, step, c, 0)
-            dneg = jnp.where(negative, jax.nn.sigmoid(logits) * (valid / BLOCK), 0.0)
-            w_high, w_low = split(jnp.where(hot, dpos, 0.0) + dneg)
-            whi[:, at] = w_high
-            wlo[:, at] = w_low
-
-    def target_grad():
-        total = jnp.zeros((width, rows), F32)
+            share = jnp.where(per_edge(nb, step, c, 0) == h, valid / BLOCK, 0.0)
+            w = jnp.where(hot, dpos, 0.0) + jax.nn.sigmoid(logits) * share
+            w_high, w_low = split(w)
+            whi[h * BLOCK : (h + 1) * BLOCK, at] = w_high
+            wlo[h * BLOCK : (h + 1) * BLOCK, at] = w_low
+
+    def target_grad(first, last):
+        total = jnp.zeros((width, last - first), F32)
         for c in range(chunks):
             at = slice(c * CHUNK, (c + 1) * CHUNK)
-            total += dot(qhi[:, at], whi[:, at], nt)
-            total += dot(qlo[:, at], whi[:, at], nt)
-            total += dot(qhi[:, at], wlo[:, at], nt)
+            total += dot(qhi[:, at], whi[first:last, at], nt)
+            total += dot(qlo[:, at], whi[first:last, at], nt)
+            total += dot(qhi[:, at], wlo[first:last, at], nt)
         return total
 
     def source_grad(step, target):
@@ -226,20 +234,25 @@
             stores.append(copy)
 
     store((expand, o_expand), (own, o_code))
-    target = None
     for step in range(steps):
         last = step == steps - 1
-        for copy in moving:
-            copy.wait()
-        target = from_wire(ubuf[step], mbuf[step, 1:2, :])
-        target_state = mbuf[step, :1, :]
-        old = target
-        weights(step, old)
+        targets, states, later = [], [], []
+        for h in range(halves):
+            for copy in moving[h]:
+                copy.wait()
+            target = from_wire(ubuf[step, h], mbuf[step, h, 1:2, :])
+            state = mbuf[step, h, :1, :]
+            weights(step, h, target)
+            targets.append(target)
+            states.append(state)
+            if not last:
+                grad = target_grad(h * BLOCK, (h + 1) * BLOCK)
+                target, state = adagrad(target, state, grad)
+                pack(step + 1, h, target, state)
+                later.append(ring(step + 1, h))
+        moving = later
+        old, target_state = jnp.concatenate(targets, axis=1), jnp.concatenate(states, axis=1)
         if not last:
-            target, target_state = adagrad(target, target_state, target_grad())
-            wire[step + 1], most = to_wire(target)
-            msend[step + 1] = jnp.where(eight == 0, target_state, most)
-            moving = ring(step + 1)
             source, source_state = adagrad(source, source_state, source_grad(step, old))
             queries(step + 1, source)
         else:
@@ -256,7 +269,7 @@
             new_src[...] = source
             new_sst[...] = source_state
             store((new_src, o_src), (new_sst, o_sst))
-            target, target_state = adagrad(target, target_state, target_grad())
+            target, target_state = adagrad(old, target_state, target_grad(0, rows))
             new_tgt[...] = target
             new_tst[...] = target_state
             store((new_tgt, o_tgt), (new_tst, o_tst))
@@ -311,6 +324,8 @@
     nrel = relation_table.shape[0]
     slots = rows // 4
     edges = blocks * BLOCK
+    halves = rows // BLOCK
+    moves = steps * halves
     hbm = pl.BlockSpec(memory_space=pltpu.HBM)
     dma = pltpu.SemaphoreType.DMA
     args = (
@@ -337,10 +352,10 @@
         scratch_shapes=[
             pltpu.VMEM(held.shape, held.dtype) for held in state + handed[5:] + args
         ] + [
-            pltpu.VMEM((steps, width, rows), jnp.int16),
-            pltpu.VMEM((steps, width, rows), jnp.int16),
-            pltpu.VMEM((steps, 8, rows), F32),
-            pltpu.VMEM((steps, 8, rows), F32),
+            pltpu.VMEM((steps, halves, width, BLOCK), jnp.int16),
+            pltpu.VMEM((steps, halves, width, BLOCK), jnp.int16),
+            pltpu.VMEM((steps, halves, 8, BLOCK), F32),
+            pltpu.VMEM((steps, halves, 8, BLOCK), F32),
             pltpu.VMEM((8, rows), F32),
             pltpu.VMEM((serve - 1, 8, rows), F32),
             pltpu.VMEM((serve - 1, slots, width), BF16),
@@ -352,7 +367,7 @@
             pltpu.VMEM((rows, edges), BF16),
             pltpu.VMEM((rows, edges), BF16),
             dma((len(args),)), dma((len(handed),)),
-            dma((steps,)), dma((steps,)), dma((steps,)), dma((steps,)),
+            dma((moves,)), dma((moves,)), dma((moves,)), dma((moves,)),
             dma((serve - 1,)), dma((serve - 1,)), dma((serve - 1,)), dma((serve - 1,)),
         ],
         compiler_params=pltpu.CompilerParams(

time: 31.6 us -> 30 us (0.949)
  Pallas kernels: 30.8 us -> 29.2 us
    pallas_call x1, Pallas kernels: 28.2 us -> 26.7 us  [on_device(): pl.pallas_call(functools.partial(kernel, dom, serve, steps, blocks), out_...]
where the time goes in v4:
time: 30 us; the launch traced here: 29.9 us
  Pallas kernels  29.2 us (97%)
  between operations  0.64 us (2%)
    pallas_call x1, Pallas kernels, on_device(): pl.pallas_call(functools.partial(kernel, dom, serve, steps, blocks), out_...  26.7 us
    pallas_call x1, Pallas kernels, on_device(): pl.pallas_call(functools.partial(finish, serve), out_shape=state + (jax.S...  2.57 us

profile of v4, /device:TPU:1, one launch (start us, length us, event | category | flops | bytes accessed | tf_op | source)
XLA Modules:
  0.0 29.9 jit_solution(17634436778069186571)
XLA Ops:
  0.6 26.7 %train.1 = (f32[400,256]{1,0:T(8,128)}, f32[1,256]{1,0:T(1,128)}, f32[400,256]{1,0:T(8,128)}, f32[1,256]{1,0:T(1,128)}, bf16[3,64,400]{2,1,0:T(8,128)(2,1)}, /*i...) custom-call(f32[400,256]{1,0:T(8,128)} %bitcast.26, f32[1,256]{1,0:T(1,128)} %bitcast.31, f32[400,256]{1,0:T(8,128)} %bitcast.27, ...), custom_call_target="tpu_custom_call" | custom-call | tf_op jit(solution)/shard_map/train/pallas_call | solution.py:347
  27.3 2.6 %publish.1 = (f32[400,256]{1,0:T(8,128)}, f32[1,256]{1,0:T(1,128)}, f32[400,256]{1,0:T(8,128)}, f32[1,256]{1,0:T(1,128)}, bf16[4,400,256]{2,1,0:T(8,128)(2,1)}) custom-call(f32[400,256]{1,0:T(8,128)} %get-tuple-element.17.refs_0_, f32[1,256]{1,0:T(1,128)} %get-tuple-element.18.refs_1_, f32[400,256]{1,0:T(8,128)} %get-tuple-element.19.refs_2_, ...), custom_call_target="tpu_custom_call" | custom-call | tf_op jit(solution)/shard_map/publish/pallas_call | solution.py:378

commit v5 on v4

--- a/solution.py
+++ b/solution.py
@@ -31,6 +31,15 @@
     return jnp.floor(u * (WIRE_MAX / most) + 0.5).astype(jnp.int32).astype(jnp.int16), most
 
 
+def stacked(x):
+    return jnp.concatenate(split(x), axis=0)
+
+
+def halves_sum(x):
+    n = x.shape[0] // 2
+    return x[:n] + x[n:]
+
+
 def from_wire(q, most):
     return q.astype(jnp.int32).astype(F32) * (most * (1.0 / WIRE_MAX))
 
@@ -49,7 +58,7 @@
     new_src, new_sst, new_tgt, new_tst, expand, own,
     src, sst, tgt, tst, rel, sid, tid, rid, nb, cnt, shard, changed,
     ubuf, wire, mbuf, msend, code, code_in, pay, pay_in, pick,
-    relg, qhi, qlo, whi, wlo,
+    relg, hots, q_parts, g_parts, whi, wlo,
     loaded, stored, u_send, u_recv, m_send, m_recv, c_send, c_recv, p_send, p_recv,
 ):
     width, rows = src.shape
@@ -63,6 +72,12 @@
     right, left = lax.rem(d + 1, dom), lax.rem(d + dom - 1, dom)
     peers = [lax.rem(s + j, serve) for j in range(1, serve)]
 
+    barrier = pltpu.get_barrier_semaphore()
+    for neighbour in (left, right):
+        pl.semaphore_signal(barrier, inc=1, device_id=(neighbour, s), device_id_type=MESH)
+    for peer in peers:
+        pl.semaphore_signal(barrier, inc=1, device_id=(d, peer), device_id_type=MESH)
+
     loads = {}
     for i, (name, given, held) in enumerate((
         ("tgt", tgt_in, tgt), ("tst", tst_in, tst), ("shard", shard_in, shard),
@@ -76,12 +91,6 @@
     def arrived(*names):
         for name in names:
             loads[name].wait()
-
-    barrier = pltpu.get_barrier_semaphore()
-    for neighbour in (left, right):
-        pl.semaphore_signal(barrier, inc=1, device_id=(neighbour, s), device_id_type=MESH)
-    for peer in peers:
-        pl.semaphore_signal(barrier, inc=1, device_id=(d, peer), device_id_type=MESH)
 
     eight = lax.broadcasted_iota(jnp.int32, (8, BLOCK), 0)
     halves = rows // BLOCK
@@ -157,51 +166,46 @@
             relg[:, at : at + CHUNK] = dot(table, ones(rel_of == ids(rid, step, c)))
 
     def queries(step, source):
-        high, low = split(source)
+        both = stacked(source)
         for c in range(chunks):
             hot = ones(one_hot(sid, step, c))
             at = (step * chunks + c) * CHUNK
-            q = (dot(high, hot) + dot(low, hot)) * relg[:, at : at + CHUNK]
-            q_high, q_low = split(q)
-            qhi[:, c * CHUNK : (c + 1) * CHUNK] = q_high
-            qlo[:, c * CHUNK : (c + 1) * CHUNK] = q_low
+            q_high, q_low = split(halves_sum(dot(both, hot)) * relg[:, at : at + CHUNK])
+            at = slice(c * CHUNK, (c + 1) * CHUNK)
+            hots[:, at] = hot
+            q_parts[:width, at] = q_high
+            q_parts[width:, at] = q_low
 
     def weights(step, h, target):
-        high, low = split(target.T)
+        both = stacked(target.T)
         for c in range(chunks):
             at = slice(c * CHUNK, (c + 1) * CHUNK)
-            a, b = qhi[:, at], qlo[:, at]
-            logits = dot(high, a) + dot(low, a) + dot(high, b)
+            logits = halves_sum(dot(both, q_parts[:width, at]))
+            logits += dot(both[:BLOCK], q_parts[width:, at])
             hot = row_of[:BLOCK] == ids(tid, step, c) - h * BLOCK
             valid = jnp.where(edge < per_edge(cnt, step, c, BLOCK), 1.0, 0.0)
             pos = jnp.sum(jnp.where(hot, logits, 0.0), axis=0, keepdims=True)
             dpos = -jax.nn.sigmoid(-pos) * valid
-            share = jnp.where(per_edge(nb, step, c, 0) == h, valid / BLOCK, 0.0)
-            w = jnp.where(hot, dpos, 0.0) + jax.nn.sigmoid(logits) * share
+            share = jnp.where(per_edge(nb, step, c, 0) == h, valid * (0.5 / BLOCK), 0.0)
+            w = jnp.where(hot, dpos + share, share) + jnp.tanh(0.5 * logits) * share
             w_high, w_low = split(w)
             whi[h * BLOCK : (h + 1) * BLOCK, at] = w_high
             wlo[h * BLOCK : (h + 1) * BLOCK, at] = w_low
 
     def target_grad(first, last):
-        total = jnp.zeros((width, last - first), F32)
+        total = halves_sum(dot(q_parts[...], whi[first:last, :], nt))
+        return total + dot(q_parts[:width, :], wlo[first:last, :], nt)
+
+    def source_grad(step, target):
+        both = stacked(target)
         for c in range(chunks):
             at = slice(c * CHUNK, (c + 1) * CHUNK)
-            total += dot(qhi[:, at], whi[first:last, at], nt)
-            total += dot(qlo[:, at], whi[first:last, at], nt)
-            total += dot(qhi[:, at], wlo[first:last, at], nt)
-        return total
-
-    def source_grad(step, target):
-        high, low = split(target)
-        total = jnp.zeros((width, rows), F32)
-        for c in range(chunks):
-            at = slice(c * CHUNK, (c + 1) * CHUNK)
-            g = dot(high, whi[:, at]) + dot(low, whi[:, at]) + dot(high, wlo[:, at])
+            g = halves_sum(dot(both, whi[:, at])) + dot(both[:width], wlo[:, at])
             r = (step * chunks + c) * CHUNK
             g_high, g_low = split(g * relg[:, r : r + CHUNK])
-            hot = ones(one_hot(sid, step, c))
-            total += dot(g_high, hot, nt) + dot(g_low, hot, nt)
-        return total
+            g_parts[:width, at] = g_high
+            g_parts[width:, at] = g_low
+        return halves_sum(dot(g_parts[...], hots[...], nt))
 
     def compaction(code_row, which):
         sel = jnp.where(code_row == which.astype(F32), 1.0, 0.0)
@@ -362,8 +366,9 @@
             pltpu.VMEM((serve - 1, slots, width), BF16),
             pltpu.VMEM((serve - 1, slots, rows), BF16),
             pltpu.VMEM((width, steps * edges), F32),
-            pltpu.VMEM((width, edges), BF16),
-            pltpu.VMEM((width, edges), BF16),
+            pltpu.VMEM((rows, edges), BF16),
+            pltpu.VMEM((2 * width, edges), BF16),
+            pltpu.VMEM((2 * width, edges), BF16),
             pltpu.VMEM((rows, edges), BF16),
             pltpu.VMEM((rows, edges), BF16),
             dma((len(args),)), dma((len(handed),)),

time: 30 us -> 30.2 us (level)
  no operation moved by 1% of the time
where the time goes in v5:
time: 30.2 us; the launch traced here: 30 us
  Pallas kernels  29.4 us (97%)
  between operations  0.64 us (2%)
    pallas_call x1, Pallas kernels, on_device(): pl.pallas_call(functools.partial(kernel, dom, serve, steps, blocks), out_...  26.8 us
    pallas_call x1, Pallas kernels, on_device(): pl.pallas_call(functools.partial(finish, serve), out_shape=state + (jax.S...  2.57 us

profile of v5, /device:TPU:1, one launch (start us, length us, event | category | flops | bytes accessed | tf_op | source)
XLA Modules:
  0.0 30.0 jit_solution(691167388915233037)
XLA Ops:
  0.6 26.8 %train.1 = (f32[400,256]{1,0:T(8,128)}, f32[1,256]{1,0:T(1,128)}, f32[400,256]{1,0:T(8,128)}, f32[1,256]{1,0:T(1,128)}, bf16[3,64,400]{2,1,0:T(8,128)(2,1)}, /*i...) custom-call(f32[400,256]{1,0:T(8,128)} %bitcast.26, f32[1,256]{1,0:T(1,128)} %bitcast.31, f32[400,256]{1,0:T(8,128)} %bitcast.27, ...), custom_call_target="tpu_custom_call" | custom-call | tf_op jit(solution)/shard_map/train/pallas_call | solution.py:351
  27.4 2.6 %publish.1 = (f32[400,256]{1,0:T(8,128)}, f32[1,256]{1,0:T(1,128)}, f32[400,256]{1,0:T(8,128)}, f32[1,256]{1,0:T(1,128)}, bf16[4,400,256]{2,1,0:T(8,128)(2,1)}) custom-call(f32[400,256]{1,0:T(8,128)} %get-tuple-element.17.refs_0_, f32[1,256]{1,0:T(1,128)} %get-tuple-element.18.refs_1_, f32[400,256]{1,0:T(8,128)} %get-tuple-element.19.refs_2_, ...), custom_call_target="tpu_custom_call" | custom-call | tf_op jit(solution)/shard_map/publish/pallas_call | solution.py:383
